TPU v7x, 32 devices: a whole 2x2x4 slice. The times are simulated.
32 devices in a mesh: seq: 8 (over y, x, core), head: 4 (over z).
Axes of the slice: x: 2, y: 2, z: 4, core: 2. Of those that a mesh axis runs over, the one named last changes fastest.
Arguments:
- queries: bfloat16 [1024, 8192], P('seq', 'head'), may hold values from -24 to 24
- key_rows: bfloat16 [1024, 1024], P('seq', 'head'), may hold values from -6 to 6
- value_rows: bfloat16 [1024, 1024], P('seq', 'head'), may hold values from -6 to 6
- out_weight: bfloat16 [8192, 8192], P('head'), may hold values from -0.5 to 0.5
- residual: bfloat16 [1024, 8192], P('seq', 'head'), may hold values from -54 to 54
- norm_gain: float32 [8192], replicated, may hold values from 0.1 to 1.9
- gate_weight: bfloat16 [8192, 28672], P(None, ('seq', 'head')), may hold values from -0.0625 to 0.0625
- up_weight: bfloat16 [8192, 28672], P(None, ('seq', 'head')), may hold values from -0.0625 to 0.0625
Outputs:
- edit_keys: bfloat16 [1024, 28672], P(None, ('seq', 'head'))
- hidden_state: bfloat16 [1024, 8192], P('seq', 'head')
All inputs are finite; a program needn't handle non-finite values.
Results may differ from a plain program's by a relative error of at most 0.019.
Values may be sent and summed in bfloat16 or wider, within the bound.
A program may use at most 128 MiB of HBM per device.

v0:
```python
import jax
import jax.numpy as jnp
from jax import lax
from jax.sharding import PartitionSpec as P

HD = 128


very_low = -1e30


def attend_block(carry_state, rows, places, key_piece, value_piece, key_places):
    maxima, totals, accumulated = carry_state
    scores = jnp.einsum(
        "rkgd,nkd->kgrn", rows, key_piece, preferred_element_type=jnp.float32
    ) / jnp.sqrt(jnp.float32(HD))
    visible = places[:, None] >= key_places[None, :]
    scores = jnp.where(visible, scores, jnp.float32(very_low))
    new_maxima = jnp.maximum(maxima, jnp.max(scores, axis=-1))
    weights = jnp.exp(scores - new_maxima[..., None])
    totals = jnp.sum(weights, axis=-1)
    products = jnp.einsum(
        "kgrn,nkd->kgrd", weights, value_piece.astype(jnp.float32), precision=lax.Precision.HIGHEST
    )
    accumulated = products
    return (new_maxima, totals, accumulated)


def maybe_attend(current, rows, places, key_piece, value_piece, key_places, first_row):

    def compute(carry_state):
        return attend_block(carry_state, rows, places, key_piece, value_piece, key_places)

    def unchanged(carry_state):
        return carry_state

    return lax.cond(first_row <= places[-1], compute, unchanged, current)


def finish_rows(carry_state, row_count, width):
    maxima, totals, accumulated = carry_state
    result = accumulated / totals[..., None]
    return result.transpose(2, 0, 1, 3).reshape(row_count, width).astype(jnp.bfloat16)


def per_device(
    queries, key_rows, value_rows, out_weight, residual, norm_gain, gate_weight, up_weight
):
    tok_count = queries.shape[0]
    seq_index = lax.axis_index("seq")
    head_index = lax.axis_index("head")
    kv_local = key_rows.shape[1] // HD
    q_local = queries.shape[1] // HD
    group_size = q_local // kv_local
    own_first = seq_index * tok_count
    query_sets = ((queries, own_first + jnp.arange(tok_count, dtype=jnp.int32)),)
    shaped = tuple(
        (
            (rows.reshape(rows.shape[0], kv_local, group_size, HD), places)
            for rows, places in query_sets
        )
    )
    initial = tuple(
        (
            (
                jnp.full((kv_local, group_size, rows.shape[0]), very_low, jnp.float32),
                jnp.zeros((kv_local, group_size, rows.shape[0]), jnp.float32),
                jnp.zeros((kv_local, group_size, rows.shape[0], HD), jnp.float32),
            )
            for rows, places in shaped
        )
    )
    first_row = jnp.int32(0)
    key_piece = lax.all_gather(key_rows, "seq", axis=0, tiled=True).reshape(-1, kv_local, HD)
    value_piece = lax.all_gather(value_rows, "seq", axis=0, tiled=True).reshape(-1, kv_local, HD)
    key_places = jnp.arange(key_piece.shape[0], dtype=jnp.int32)
    updated = []
    for (fold_rows, fold_places), current in zip(shaped, initial):
        updated.append(
            maybe_attend(
                current, fold_rows, fold_places, key_piece, value_piece, key_places, first_row
            )
        )
    final_states = tuple(updated)
    finished = [
        finish_rows(state, rows.shape[0], q_local * HD)
        for state, (rows, places) in zip(final_states, shaped)
    ]
    attended = finished[0]
    projected = jnp.dot(attended, out_weight, preferred_element_type=jnp.float32)
    width_total = out_weight.shape[1]
    width_local = residual.shape[1]
    column_first = head_index * width_local
    placed = lax.dynamic_update_slice_in_dim(
        jnp.zeros((tok_count, width_total), jnp.float32),
        residual.astype(jnp.float32),
        column_first,
        1,
    )
    summed = lax.psum((projected + placed).astype(jnp.bfloat16), "head")
    hidden_state = lax.dynamic_slice_in_dim(summed, column_first, width_local, 1)
    widened = summed.astype(jnp.float32)
    mean_square = jnp.sum(widened * widened, axis=-1, keepdims=True) / width_total
    normed_full = (widened * lax.rsqrt(mean_square + 1e-05) * norm_gain[None, :]).astype(
        jnp.bfloat16
    )
    shard_rows = lax.all_gather(normed_full, "seq", axis=0, tiled=True)
    gate_sums = jnp.dot(shard_rows, gate_weight, preferred_element_type=jnp.float32)
    up_sums = jnp.dot(shard_rows, up_weight, preferred_element_type=jnp.float32)
    edit_keys = (jax.nn.silu(gate_sums) * up_sums).astype(jnp.bfloat16)
    return (edit_keys, hidden_state)


def solution(mesh):
    return jax.shard_map(
        per_device,
        mesh=mesh,
        in_specs=(
            P("seq", "head"),
            P("seq", "head"),
            P("seq", "head"),
            P("head", None),
            P("seq", "head"),
            P(),
            P(None, ("seq", "head")),
            P(None, ("seq", "head")),
        ),
        out_specs=(P(None, ("seq", "head")), P("seq", "head")),
        check_vma=False,
    )
```

profile of v0, /device:TPU:7, one launch (start us, length us, event | category | flops | bytes accessed | tf_op | source)
XLA Modules:
  0.0 283.0 jit_solution(17613547794899008051)
XLA Ops:
  7.2 0.0 all-reduce.2.cloned.1.call-start
  7.2 0.6 slice.3
  8.5 9.7 %all_gather.9 = bf16[1024,256]{1,0:T(8,128)(2,1)S(1)} all-gather(bf16[128,256]{1,0:T(8,128)(2,1)} %param.11), channel_id=1, replica_groups=mesh['seq'=8,'head'=4] {'seq'}, dimensions={0}, use_global_device_ids=true | all-gather | bytes 589824 | tf_op jit(solution)/shard_map/all_gather | solution.py:74
  18.2 9.5 %all_gather.10 = bf16[1024,256]{1,0:T(8,128)(2,1)S(1)} all-gather(bf16[128,256]{1,0:T(8,128)(2,1)} %param.12), channel_id=1, replica_groups=mesh['seq'=8,'head'=4] {'seq'}, dimensions={0}, use_global_device_ids=true | all-gather | bytes 589824 | tf_op jit(solution)/shard_map/all_gather | solution.py:75
  27.7 9.6 %conditional.1 = (f32[2,8,128]{2,1,0:T(8,128)S(1)}, f32[2,8,128,128]{2,3,1,0:T(8,128)S(1)}) conditional(s32[]{:T(128)} %bitcast.3, () %tuple.16, (s32[128]{0:T(128)S(1)}, s32[1024]{0:T(1024)S(1)}, bf16[1024,256]{1,0:T(8,128)(2,1)S(1)}, bf16[128,2048]{1,0:T(8,128)(2,1)}, bf16[1024,256]{1,0:T(8,128)(2,1)S(1)}) %tuple.17), branch_computations={%region_0.0_spmd, %region_1.4_spmd} | conditional | flops 3779196928 | bytes 31511056 | solution.py:37
  27.7 0.2 broadcast_compare_fusion
  27.9 0.1 reshape.34
  28.0 1.1 copy.29
  29.2 0.1 reshape.36
  29.3 1.4 fusion.2
  30.7 1.7 fusion.1
  32.4 4.6 %fusion = f32[2,8,128,128]{2,3,1,0:T(8,128)S(1)} fusion(f32[2,1024,128,8]{2,1,3,0:T(8,128)S(1)} %get-tuple-element.28, f32[2,8,128]{2,1,0:T(8,128)S(1)} %broadcast_maximum_fusion, pred[128,1024]{0,1:T(8,128)(4,1)S(1)} %broadcast_compare_fusion, bf16[1024,2,128,1]{2,1,0,3:T(2,128)(2,1)S(1)} %bitcast.28), kind=kOutput, calls=%fused_computation.2 | convolution fusion | flops 3227516928 | bytes 10100736 | tf_op jit(solution)/shard_map/cond | solution.py:37
  37.3 0.1 divide_convert_fusion
  37.4 0.0 copy-start
  37.4 13.0 %fusion.16 = f32[128,8192]{1,0:T(8,128)S(1)} fusion(bf16[128,2048]{0,1:T(8,128)(2,1)S(1)} %bitcast.25, bf16[2048,8192]{1,0:T(8,128)(2,1)} %param.13), kind=kOutput, calls=%fused_computation.28 | convolution fusion | flops 4294967296 | bytes 38273024 | tf_op jit(solution)/shard_map/dot_general | solution.py:90
  50.4 0.0 copy-done
  50.4 0.0 copy-start.1
  50.4 0.2 add_dynamic-update-slice_fusion
  50.6 1.6 convert_element_type.37
  52.2 0.0 all-reduce.2.cloned.1.call-update
  52.2 0.0 all-gather.2.cloned.1.call-start
  52.3 87.3 %all-reduce.2.cloned.1.call-done = bf16[128,8192]{1,0:T(8,128)(2,1)} async-done(((bf16[128,8192]{1,0:T(8,128)(2,1)}), bf16[128,8192]{1,0:T(8,128)(2,1)}) %all-reduce.2.cloned.1.call-update) | async-done | bytes 2097168 | tf_op jit(solution)/shard_map/psum | solution.py:100
  139.6 2.1 fusion.13
  141.7 0.0 copy-done.1
  141.7 3.5 %fusion.15 = bf16[128,8192]{1,0:T(8,128)(2,1)} fusion(bf16[128,8192]{1,0:T(8,128)(2,1)} %all-reduce.2.cloned.1.call-done, f32[8192]{0:T(1024)S(1)} %copy-done.1, f32[128]{0:T(128)S(1)} %add_rsqrt_fusion), kind=kLoop, calls=%fused_computation.21 | loop fusion | flops 4194304 | bytes 4227584 | tf_op jit(solution)/shard_map/convert_element_type | solution.py:104
  145.2 0.0 all-gather.2.cloned.1.call-update
  145.2 1.9 constant_dynamic-slice_fusion
  147.1 86.6 %all-gather.2.cloned.1.call-done = bf16[1024,8192]{1,0:T(8,128)(2,1)} async-done(((bf16[128,8192]{1,0:T(8,128)(2,1)}), bf16[1024,8192]{1,0:T(8,128)(2,1)}) %all-gather.2.cloned.1.call-update) | async-done | bytes 16777232 | tf_op jit(solution)/shard_map/all_gather | solution.py:107
  233.7 0.0 copy-start.2
  233.7 21.4 %fusion.17 = f32[1024,896]{1,0:T(8,128)S(1)} fusion(bf16[1024,8192]{1,0:T(8,128)(2,1)} %all-gather.2.cloned.1.call-done, bf16[8192,896]{1,0:T(8,128)(2,1)} %param.16), kind=kOutput, calls=%fused_computation.29 | convolution fusion | flops 15032385536 | bytes 35127296 | tf_op jit(solution)/shard_map/dot_general | solution.py:108
  255.1 0.0 copy-done.2
  255.1 21.0 %multiply_convert_fusion = bf16[1024,896]{1,0:T(8,128)(2,1)} fusion(f32[1024,896]{1,0:T(8,128)S(1)} %fusion.17, bf16[1024,8192]{1,0:T(8,128)(2,1)S(1)} %copy-done.2, bf16[8192,896]{1,0:T(8,128)(2,1)} %param.17), kind=kOutput, calls=%fused_computation.22 | convolution fusion | flops 15037890560 | bytes 36962304 | tf_op jit(solution)/shard_map/dot_general | solution.py:109
  (4 shorter events, 0.0 us)
Async XLA Ops:
  7.2 132.4 %all-reduce.2.cloned.1.call-start = ((), (), s32[]{:S(2)}) async-start(), calls=%async_computation | async-start | bytes 4194304 | tf_op jit(solution)/shard_map/psum | solution.py:100
  37.4 13.0 %copy-start = (bf16[128,2048]{1,0:T(8,128)(2,1)S(1)}, bf16[128,2048]{1,0:T(8,128)(2,1)}, u32[]{:S(2)}) copy-start(bf16[128,2048]{1,0:T(8,128)(2,1)} %param.14) | copy-start | bytes 1572868
  50.4 91.3 %copy-start.1 = (f32[8192]{0:T(1024)S(1)}, f32[8192]{0:T(1024)}, u32[]{:S(2)}) copy-start(f32[8192]{0:T(1024)} %param.15) | copy-start | bytes 98308
  52.2 181.4 %all-gather.2.cloned.1.call-start = ((), (), s32[]{:S(2)}) async-start(), calls=%async_computation.1 | async-start | bytes 18874368 | tf_op jit(solution)/shard_map/all_gather | solution.py:107
  233.7 21.5 %copy-start.2 = (bf16[1024,8192]{1,0:T(8,128)(2,1)S(1)}, bf16[1024,8192]{1,0:T(8,128)(2,1)}, u32[]{:S(2)}) copy-start(bf16[1024,8192]{1,0:T(8,128)(2,1)} %all-gather.2.cloned.1.call-done) | copy-start | bytes 50331652
Sparse Core Ops, SparseCore 0:
  52.4 87.1 all-reduce.1
  145.3 88.3 all-gather.1
where the time goes:
time: 285 us; the launch traced here: 283 us
  waiting for transfers between devices  174 us (61%)
  matrix products  61.5 us (22%)
  blocking collectives  19.2 us (7%)
  between operations  14.8 us (5%)
  other arithmetic  9.37 us (3%)
  local copies, waits for them, and re-layouts  3.89 us (1%)
    psum x1, waiting for transfers between devices, per_device(): summed = lax.psum((projected + placed).astype(jnp.bfloat16), 'head')  87.3 us
    all_gather x1, waiting for transfers between devices, per_device(): shard_rows = lax.all_gather(normed_full, 'seq', axis=0, tiled=True)  86.6 us
    dot_general x1, matrix products, per_device(): jnp.dot(shard_rows, gate_weight, preferred_element_type=jnp.float32)  21.4 us
    dot_general x1, matrix products, per_device(): up_sums = jnp.dot(shard_rows, up_weight, preferred_element_type=jnp.float32)  21 us
    dot_general x1, matrix products, per_device(): jnp.dot(attended, out_weight, preferred_element_type=jnp.float32)  13 us
    all_gather x1, blocking collectives, per_device(): lax.all_gather(key_rows, 'seq', axis=0, tiled=True)  9.69 us
    all_gather x1, blocking collectives, per_device(): lax.all_gather(value_rows, 'seq', axis=0, tiled=True)  9.53 us
  transfers between devices with their start and end apart: 2, of which 2 were waited for; matrix products, arithmetic and copies ran while one was open for 1% of the time, Pallas kernels for 0%

commit v1 on v0

v1 whole, which is shorter than its diff:
```python
import functools
import jax
import jax.numpy as jnp
from jax import lax
from jax.experimental import pallas as pl
from jax.experimental.pallas import tpu as pltpu
from jax.sharding import PartitionSpec as P

HD = 128
MESH = pl.DeviceIdType.MESH
VMEM_LIMIT = 60 * 1024 * 1024


very_low = -1e30


def chip_at(place):
    return (place // 2) * 2 + (place % 2 + place // 2) % 2


def gather_kernel(
    n_s, n_h, x_in, gate_hbm, up_hbm, out_ref,
    x, gate_w, up_w, acc, net_sem, sib_sem, send_sem, weight_sem,
):
    seq = lax.axis_index("seq")
    z = lax.axis_index("head")
    rows, cols = x_in.shape
    hidden = gate_hbm.shape[1]
    n_c = n_s // 2
    half = n_c // 2
    core = seq % 2
    chip = seq // 2
    sibling = chip * 2 + 1 - core
    place = chip_at(chip)
    right = chip_at((place + 1) % n_c) * 2 + core
    left = chip_at((place + n_c - 1) % n_c) * 2 + core
    has_up = z + 1 < n_h
    has_down = z > 0
    short = jnp.minimum(z, n_h - 1 - z)

    def part_of(rank):
        near = z + ((rank + 1) // 2) * (1 - 2 * (rank % 2))
        far = jnp.where(z == short, rank, n_h - 1 - rank)
        return jnp.where(rank <= 2 * short, near, far)

    barrier = pltpu.get_barrier_semaphore()
    for other in (sibling, right, left):
        pl.semaphore_signal(barrier, inc=1, device_id=(other, z), device_id_type=MESH)

    @pl.when(has_up)
    def _():
        pl.semaphore_signal(barrier, inc=1, device_id=(seq, z + 1), device_id_type=MESH)

    @pl.when(has_down)
    def _():
        pl.semaphore_signal(barrier, inc=1, device_id=(seq, z - 1), device_id_type=MESH)

    def weight_copies(part):
        depth = pl.ds(pl.multiple_of(part * cols, cols), cols)
        return (
            pltpu.make_async_copy(gate_hbm.at[depth], gate_w.at[depth], weight_sem.at[0, part]),
            pltpu.make_async_copy(up_hbm.at[depth], up_w.at[depth], weight_sem.at[1, part]),
        )

    @pl.loop(0, n_h)
    def _(rank):
        for copy in weight_copies(part_of(rank)):
            copy.start()

    def block(source, owner_core, part):
        first = pl.multiple_of((source * 2 + owner_core) * rows, rows)
        return x.at[part, pl.ds(first, rows), :]

    def to(way, source, part, target, sems):
        held = block(source, core, part)
        return pltpu.make_async_remote_copy(
            src_ref=held,
            dst_ref=held,
            send_sem=send_sem.at[way, source, part],
            recv_sem=sems.at[source, part],
            device_id=target,
            device_id_type=MESH,
        )

    def unit(step, turn):
        distance = (turn + 1) // 2
        rank = step - distance
        valid = jnp.logical_and(rank >= 0, rank < n_h)
        safe = jnp.clip(rank, 0, n_h - 1)
        part = part_of(safe)
        source = chip_at((place + n_c + distance * (1 - 2 * (turn % 2))) % n_c)
        return distance, rank, valid, part, source

    def sends(step, turn, act):
        distance, rank, valid, part, source = unit(step, turn)
        own = turn == 0
        last_right = part % 2 == 0
        onward = distance + 1
        from_left = turn % 2 == 1
        more_right = jnp.logical_or(onward < half, jnp.logical_and(onward == half, last_right))
        more_left = jnp.logical_or(
            onward < half, jnp.logical_and(onward == half, jnp.logical_not(last_right))
        )
        go_right = jnp.logical_or(own, jnp.logical_and(from_left, more_right))
        go_left = jnp.logical_or(own, jnp.logical_and(jnp.logical_not(from_left), more_left))
        go_up = jnp.logical_and(own, jnp.logical_and(part <= z, has_up))
        go_down = jnp.logical_and(own, jnp.logical_and(part >= z, has_down))

        @pl.when(jnp.logical_and(valid, go_up))
        def _():
            act(to(0, source, part, (seq, z + 1), net_sem))

        @pl.when(jnp.logical_and(valid, go_down))
        def _():
            act(to(1, source, part, (seq, z - 1), net_sem))

        @pl.when(jnp.logical_and(valid, go_right))
        def _():
            act(to(2, source, part, (right, z), net_sem))

        @pl.when(jnp.logical_and(valid, go_left))
        def _():
            act(to(3, source, part, (left, z), net_sem))

        @pl.when(valid)
        def _():
            act(to(4, source, part, (sibling, z), sib_sem))

    first = pl.multiple_of(seq * rows, rows)
    x[z, pl.ds(first, rows), :] = x_in[...]
    neighbours = 3 + has_up.astype(jnp.int32) + has_down.astype(jnp.int32)
    pl.semaphore_wait(barrier, neighbours)

    steps = n_h + half

    @pl.loop(0, steps)
    def _(step):
        @pl.loop(0, n_c)
        def _(turn):
            distance, rank, valid, part, source = unit(step, turn)

            @pl.when(jnp.logical_and(valid, step > 0))
            def _():
                to(2, source, part, (right, z), net_sem).wait_recv()

            sends(step, turn, lambda copy: copy.start())

        @pl.loop(0, n_c)
        def _(turn):
            distance, rank, valid, part, source = unit(step, turn)

            @pl.when(jnp.logical_and(valid, turn == 0))
            def _():
                for copy in weight_copies(part):
                    copy.wait()

            @pl.when(valid)
            def _():
                other = block(source, 1 - core, part)
                pltpu.make_async_remote_copy(
                    src_ref=other,
                    dst_ref=other,
                    send_sem=send_sem.at[4, source, part],
                    recv_sem=sib_sem.at[source, part],
                    device_id=(sibling, z),
                    device_id_type=MESH,
                ).wait_recv()
                start = pl.multiple_of(source * 2 * rows, 2 * rows)
                here = pl.ds(start, 2 * rows)
                depth = pl.ds(pl.multiple_of(part * cols, cols), cols)
                features = x[part, here, :]
                gate = jnp.dot(features, gate_w[depth, :], preferred_element_type=jnp.float32)

                @pl.when(rank == 0)
                def _():
                    acc[0, here, :] = gate

                @pl.when(rank > 0)
                def _():
                    acc[0, here, :] += gate

                up = jnp.dot(features, up_w[depth, :], preferred_element_type=jnp.float32)

                @pl.when(rank == 0)
                def _():
                    acc[1, here, :] = up

                @pl.when(rank > 0)
                def _():
                    acc[1, here, :] += up

            @pl.when(rank == n_h - 1)
            def _():
                start = pl.multiple_of(source * 2 * rows, 2 * rows)
                here = pl.ds(start, 2 * rows)
                gate = acc[0, here, :]
                out_ref[here, :] = (gate / (1.0 + jnp.exp(-gate)) * acc[1, here, :]).astype(
                    out_ref.dtype
                )

    @pl.loop(0, steps)
    def _(step):
        @pl.loop(0, n_c)
        def _(turn):
            sends(step, turn, lambda copy: copy.wait_send())


def gathered_keys(n_s, n_h, normed, gate_weight, up_weight):
    rows, cols = normed.shape
    tokens = n_s * rows
    width, hidden = gate_weight.shape
    n_c = n_s // 2
    return pl.pallas_call(
        functools.partial(gather_kernel, n_s, n_h),
        out_shape=jax.ShapeDtypeStruct((tokens, hidden), jnp.bfloat16),
        in_specs=[
            pl.BlockSpec(memory_space=pltpu.VMEM),
            pl.BlockSpec(memory_space=pl.ANY),
            pl.BlockSpec(memory_space=pl.ANY),
        ],
        out_specs=pl.BlockSpec(memory_space=pltpu.VMEM),
        scratch_shapes=[
            pltpu.VMEM((n_h, tokens, cols), jnp.bfloat16),
            pltpu.VMEM((width, hidden), jnp.bfloat16),
            pltpu.VMEM((width, hidden), jnp.bfloat16),
            pltpu.VMEM((2, tokens, hidden), jnp.float32),
            pltpu.SemaphoreType.DMA((n_c, n_h)),
            pltpu.SemaphoreType.DMA((n_c, n_h)),
            pltpu.SemaphoreType.DMA((5, n_c, n_h)),
            pltpu.SemaphoreType.DMA((2, n_h)),
        ],
        compiler_params=pltpu.CompilerParams(
            collective_id=0, has_side_effects=True, vmem_limit_bytes=VMEM_LIMIT
        ),
        cost_estimate=pl.CostEstimate(
            flops=4 * tokens * width * hidden,
            bytes_accessed=4 * width * hidden,
            transcendentals=tokens * hidden,
        ),
        name="gather_and_project",
    )(normed, gate_weight, up_weight)


def attend(rows, places, key_piece, value_piece, key_places):
    scores = jnp.einsum(
        "rkgd,nkd->kgrn", rows, key_piece, preferred_element_type=jnp.float32
    ) / jnp.sqrt(jnp.float32(HD))
    visible = places[:, None] >= key_places[None, :]
    scores = jnp.where(visible, scores, jnp.float32(very_low))
    maxima = jnp.max(scores, axis=-1)
    weights = jnp.exp(scores - maxima[..., None])
    totals = jnp.sum(weights, axis=-1)
    products = jnp.einsum(
        "kgrn,nkd->kgrd", weights, value_piece.astype(jnp.float32), precision=lax.Precision.HIGHEST
    )
    result = products / totals[..., None]
    row_count = rows.shape[0]
    return result.transpose(2, 0, 1, 3).reshape(row_count, -1).astype(jnp.bfloat16)


def per_device(
    n_s, n_h, queries, key_rows, value_rows, out_weight, residual, norm_gain, gate_weight, up_weight
):
    tok_count = queries.shape[0]
    seq_index = lax.axis_index("seq")
    head_index = lax.axis_index("head")
    kv_local = key_rows.shape[1] // HD
    q_local = queries.shape[1] // HD
    group_size = q_local // kv_local
    places = seq_index * tok_count + jnp.arange(tok_count, dtype=jnp.int32)
    both = lax.all_gather(
        jnp.concatenate([key_rows, value_rows], axis=1), "seq", axis=0, tiled=True
    )
    width = key_rows.shape[1]
    key_piece = both[:, :width].reshape(-1, kv_local, HD)
    value_piece = both[:, width:].reshape(-1, kv_local, HD)
    key_places = jnp.arange(key_piece.shape[0], dtype=jnp.int32)
    attended = attend(
        queries.reshape(tok_count, kv_local, group_size, HD),
        places, key_piece, value_piece, key_places,
    )
    projected = jnp.dot(attended, out_weight, preferred_element_type=jnp.float32)
    width_total = out_weight.shape[1]
    width_local = residual.shape[1]
    column_first = head_index * width_local
    summed = lax.psum_scatter(
        projected.astype(jnp.bfloat16), "head", scatter_dimension=1, tiled=True
    )
    hidden_state = (summed.astype(jnp.float32) + residual.astype(jnp.float32)).astype(jnp.bfloat16)
    widened = hidden_state.astype(jnp.float32)
    mean_square = (
        lax.psum(jnp.sum(widened * widened, axis=-1, keepdims=True), "head") / width_total
    )
    gain = lax.dynamic_slice_in_dim(norm_gain, column_first, width_local, 0)
    normed = (widened * lax.rsqrt(mean_square + 1e-05) * gain[None, :]).astype(jnp.bfloat16)
    edit_keys = gathered_keys(n_s, n_h, normed, gate_weight, up_weight)
    return (edit_keys, hidden_state)


def solution(mesh):
    return jax.shard_map(
        functools.partial(per_device, mesh.shape["seq"], mesh.shape["head"]),
        mesh=mesh,
        in_specs=(
            P("seq", "head"),
            P("seq", "head"),
            P("seq", "head"),
            P("head", None),
            P("seq", "head"),
            P(),
            P(None, ("seq", "head")),
            P(None, ("seq", "head")),
        ),
        out_specs=(P(None, ("seq", "head")), P("seq", "head")),
        check_vma=False,
    )
```

time: 285 us -> 228 us (0.80)
  waiting for transfers between devices: 174 us -> 67.3 us
  Pallas kernels: 0 us -> 102 us
  matrix products: 61.5 us -> 23 us
  blocking collectives: 19.2 us -> 8.43 us
  other arithmetic: 9.37 us -> 4.79 us
  local copies, waits for them, and re-layouts: 3.89 us -> 7.9 us
    pallas_call x0 -> x1, Pallas kernels: none -> 102 us  [gathered_keys(): pl.pallas_call(functools.partial(gather_kernel, n_s, n_h), out_shape=jax....]
    psum x1 -> x0, waiting for transfers between devices: 87.3 us -> none  [per_device(): summed = lax.psum((projected + placed).astype(jnp.bfloat16), 'head')]
    all_gather x1, waiting for transfers between devices: 86.6 us -> 23.6 us  [per_device(): lax.all_gather(jnp.concatenate([key_rows, value_rows], axis=1), 'seq', ax...]
    reduce_scatter x0 -> x1, waiting for transfers between devices: none -> 43.6 us  [per_device(): lax.psum_scatter(projected.astype(jnp.bfloat16), 'head', scatter_dimensio...]
    dot_general x3 -> x2, matrix products: 43.9 us -> 6.14 us  [the longest x1 4.65 us: attend(): jnp.einsum('kgrn,nkd->kgrd', weights, value_piece.astype(jnp.float32), pr...]
    all_gather x2 -> x0, blocking collectives: 19.2 us -> none  [the longest x1 9.69 us: per_device(): lax.all_gather(key_rows, 'seq', axis=0, tiled=True)]
    psum x0 -> x1, blocking collectives: none -> 8.43 us  [per_device(): lax.psum(jnp.sum(widened * widened, axis=-1, keepdims=True), 'head')]
    unnamed x6 -> x8, local copies, waits for them, and re-layouts: 0.02 us -> 5.93 us
where the time goes in v1:
time: 228 us
  Pallas kernels  102 us (45%)
  waiting for transfers between devices  67.3 us (30%)
  matrix products  23 us (10%)
  between operations  14.1 us (6%)
  blocking collectives  8.43 us (4%)
  local copies, waits for them, and re-layouts  7.9 us (3%)
  other arithmetic  4.79 us (2%)
    pallas_call x1, Pallas kernels, gathered_keys(): pl.pallas_call(functools.partial(gather_kernel, n_s, n_h), out_shape=jax....  102 us
    reduce_scatter x1, waiting for transfers between devices, per_device(): lax.psum_scatter(projected.astype(jnp.bfloat16), 'head', scatter_dimensio...  43.6 us
    all_gather x1, waiting for transfers between devices, per_device(): lax.all_gather(jnp.concatenate([key_rows, value_rows], axis=1), 'seq', ax...  23.6 us
    dot_general x1, matrix products, per_device(): jnp.dot(attended, out_weight, preferred_element_type=jnp.float32)  16.8 us
    psum x1, blocking collectives, per_device(): lax.psum(jnp.sum(widened * widened, axis=-1, keepdims=True), 'head')  8.43 us
    unnamed x8, local copies, waits for them, and re-layouts  5.93 us
    dot_general x1, matrix products, attend(): jnp.einsum('kgrn,nkd->kgrd', weights, value_piece.astype(jnp.float32), pr...  4.65 us
  transfers between devices with their start and end apart: 2, of which 2 were waited for; matrix products, arithmetic and copies ran while one was open for 1% of the time, Pallas kernels for 0%

profile of v1, /device:TPU:7, one launch (start us, length us, event | category | flops | bytes accessed | tf_op | source)
XLA Modules:
  0.0 227.6 jit_solution(11422534699715296793)
XLA Ops:
  7.2 0.0 all-gather.2.cloned.1.call-start
  7.2 0.9 copy.14
  8.2 1.0 copy.13
  9.1 0.7 pad_maximum_fusion
  9.8 0.0 all-gather.2.cloned.1.call-update
  9.8 0.0 reduce-scatter.2.cloned.1.call-start
  9.9 1.1 copy.23
  11.0 0.1 iota_compare_fusion
  11.1 23.6 %all-gather.2.cloned.1.call-done = bf16[1024,512]{0,1:T(8,128)(2,1)} async-done(((bf16[128,512]{0,1:T(8,128)(2,1)}), bf16[1024,512]{0,1:T(8,128)(2,1)}) %all-gather.2.cloned.1.call-update) | async-done | bytes 1048592 | tf_op jit(solution)/shard_map/all_gather | solution.py:271
  34.7 1.3 fusion.15
  36.0 1.5 fusion.2
  37.5 1.7 fusion
  39.2 4.7 %divide_convert_fusion = bf16[128,2,8,128]{0,3,2,1:T(8,128)(2,1)S(1)} fusion(bf16[1024,2,128,1]{0,2,3,1:T(8,128)(2,1)S(1)} %bitcast.43, f32[2,1024,128,8]{2,1,3,0:T(8,128)S(1)} %get-tuple-element.7, f32[2,8,128]{2,1,0:T(8,128)S(1)} %get-tuple-element.6, pred[128,1024]{0,1:T(8,128)(4,1)S(1)} %iota_compare_fusion, f32[128,2,8]{0,2,1:T(8,128)S(1)} %bitcast.44), kind=kOutput, calls=%fused_computation.17 | convolution fusion | flops 3228041216 | bytes 9584640 | tf_op jit(solution)/shard_map/kgrn,nkd->kgrd/dot_general | solution.py:253
  43.9 0.0 copy-start.1
  43.9 16.8 %convolution_convert_fusion = bf16[128,8192]{1,0:T(8,128)(2,1)} fusion(bf16[128,2048]{0,1:T(8,128)(2,1)S(1)} %bitcast.41, bf16[2048,8192]{1,0:T(8,128)(2,1)} %param.11), kind=kOutput, calls=%fused_computation | convolution fusion | flops 4296015872 | bytes 36175872 | tf_op jit(solution)/shard_map/dot_general | solution.py:282
  60.7 0.0 reduce-scatter.2.cloned.1.call-update
  60.8 0.7 dynamic_slice.3
  61.5 43.6 %reduce-scatter.2.cloned.1.call-done = bf16[128,2048]{1,0:T(8,128)(2,1)} async-done(((bf16[128,8192]{1,0:T(8,128)(2,1)}), bf16[128,2048]{1,0:T(8,128)(2,1)}) %reduce-scatter.2.cloned.1.call-update) | async-done | bytes 524304 | tf_op jit(solution)/shard_map/reduce_scatter | solution.py:286
  105.1 0.0 copy-done.1
  105.1 1.3 fusion.8
  106.4 0.0 copy-start
  106.4 8.4 %psum.7 = f32[128,1]{0,1:T(1,128)S(1)} all-reduce(f32[128,1]{0,1:T(1,128)S(1)} %bitcast.45), channel_id=1, replica_groups=mesh['seq'=8,'head'=4] {'head'}, use_global_device_ids=true, to_apply=%region_4.5 | all-reduce | flops 128 | bytes 1024 | tf_op jit(solution)/shard_map/psum | solution.py:292
  114.9 1.0 fusion.10.x_in
  115.8 102.0 %gather_and_project.1 = bf16[1024,896]{1,0:T(8,128)(2,1)} custom-call(bf16[128,2048]{1,0:T(8,128)(2,1)} %fusion.10.x_in, bf16[8192,896]{1,0:T(8,128)(2,1)} %gate_hbm.1, bf16[8192,896]{1,0:T(8,128)(2,1)} %up_hbm.1), custom_call_target="tpu_custom_call" | custom-call | flops 30064771072 | bytes 29360128 | tf_op jit(solution)/shard_map/gather_and_project/pallas_call | solution.py:213
  217.9 0.0 copy-done
  217.9 2.9 %copy.29 = bf16[1024,896]{1,0:T(8,128)(2,1)} copy(bf16[1024,896]{1,0:T(8,128)(2,1)} %gather_and_project.1) | data formatting | bytes 3670016
  (2 shorter events, 0.0 us)
Async XLA Ops:
  7.2 27.6 %all-gather.2.cloned.1.call-start = ((), (), s32[]{:S(2)}) async-start(), calls=%async_computation.1 | async-start | bytes 1179648 | tf_op jit(solution)/shard_map/all_gather | solution.py:271
  9.8 95.3 %reduce-scatter.2.cloned.1.call-start = ((), (), s32[]{:S(2)}) async-start(), calls=%async_computation.2 | async-start | bytes 2621440 | tf_op jit(solution)/shard_map/reduce_scatter | solution.py:286
  43.9 61.2 %copy-start.1 = (bf16[128,2048]{1,0:T(8,128)(2,1)S(1)}, bf16[128,2048]{1,0:T(8,128)(2,1)}, u32[]{:S(2)}) copy-start(bf16[128,2048]{1,0:T(8,128)(2,1)} %param.12) | copy-start | bytes 1572868
  106.4 111.5 %copy-start = (bf16[128,2048]{1,0:T(8,128)(2,1)}, bf16[128,2048]{1,0:T(8,128)(2,1)S(1)}, u32[]{:S(2)}) copy-start(bf16[128,2048]{1,0:T(8,128)(2,1)S(1)} %get-tuple-element.11) | copy-start | bytes 1572868
Sparse Core Ops, SparseCore 0:
  10.4 24.2 all-gather.1
  60.9 44.1 reduce-scatter.1

commit v2 on v1

--- a/solution.py
+++ b/solution.py
@@ -251,7 +251,10 @@
     weights = jnp.exp(scores - maxima[..., None])
     totals = jnp.sum(weights, axis=-1)
     products = jnp.einsum(
-        "kgrn,nkd->kgrd", weights, value_piece.astype(jnp.float32), precision=lax.Precision.HIGHEST
+        "kgrn,nkd->kgrd",
+        weights.astype(jnp.bfloat16),
+        value_piece,
+        preferred_element_type=jnp.float32,
     )
     result = products / totals[..., None]
     row_count = rows.shape[0]
@@ -268,12 +271,8 @@
     q_local = queries.shape[1] // HD
     group_size = q_local // kv_local
     places = seq_index * tok_count + jnp.arange(tok_count, dtype=jnp.int32)
-    both = lax.all_gather(
-        jnp.concatenate([key_rows, value_rows], axis=1), "seq", axis=0, tiled=True
-    )
-    width = key_rows.shape[1]
-    key_piece = both[:, :width].reshape(-1, kv_local, HD)
-    value_piece = both[:, width:].reshape(-1, kv_local, HD)
+    key_piece = lax.all_gather(key_rows, "seq", axis=0, tiled=True).reshape(-1, kv_local, HD)
+    value_piece = lax.all_gather(value_rows, "seq", axis=0, tiled=True).reshape(-1, kv_local, HD)
     key_places = jnp.arange(key_piece.shape[0], dtype=jnp.int32)
     attended = attend(
         queries.reshape(tok_count, kv_local, group_size, HD),
@@ -288,9 +287,7 @@
     )
     hidden_state = (summed.astype(jnp.float32) + residual.astype(jnp.float32)).astype(jnp.bfloat16)
     widened = hidden_state.astype(jnp.float32)
-    mean_square = (
-        lax.psum(jnp.sum(widened * widened, axis=-1, keepdims=True), "head") / width_total
-    )
+    mean_square = (lax.psum(jnp.sum(widened * widened, axis=-1), "head") / width_total)[:, None]
     gain = lax.dynamic_slice_in_dim(norm_gain, column_first, width_local, 0)
     normed = (widened * lax.rsqrt(mean_square + 1e-05) * gain[None, :]).astype(jnp.bfloat16)
     edit_keys = gathered_keys(n_s, n_h, normed, gate_weight, up_weight)

time: 228 us -> 219 us (0.961)
  waiting for transfers between devices: 67.3 us -> 43.9 us
  blocking collectives: 8.43 us -> 27.6 us
  matrix products: 23 us -> 20.5 us
    all_gather x1 -> x0, waiting for transfers between devices: 23.6 us -> none  [per_device(): lax.all_gather(jnp.concatenate([key_rows, value_rows], axis=1), 'seq', ax...]
    all_gather x0 -> x2, blocking collectives: none -> 19.4 us  [the longest x1 9.84 us: per_device(): lax.all_gather(value_rows, 'seq', axis=0, tiled=True)]
    dot_general x1, matrix products: 4.65 us -> 2.17 us  [attend(): jnp.einsum('kgrn,nkd->kgrd', weights.astype(jnp.bfloat16), value_piece, p...]
    unnamed x8 -> x7, local copies, waits for them, and re-layouts: 5.93 us -> 4.98 us
  transfers between devices with their start and end apart: 2 -> 1, of which waited for: 2 -> 1; matrix products, arithmetic and copies ran while one was open for 1% -> 0% of each run, Pallas kernels for 0% -> 0%
where the time goes in v2:
time: 219 us; the launch traced here: 218 us
  Pallas kernels  102 us (47%)
  waiting for transfers between devices  43.9 us (20%)
  blocking collectives  27.6 us (13%)
  matrix products  20.5 us (9%)
  between operations  14.1 us (6%)
  local copies, waits for them, and re-layouts  5.89 us (3%)
  other arithmetic  4.14 us (2%)
    pallas_call x1, Pallas kernels, gathered_keys(): pl.pallas_call(functools.partial(gather_kernel, n_s, n_h), out_shape=jax....  102 us
    reduce_scatter x1, waiting for transfers between devices, per_device(): lax.psum_scatter(projected.astype(jnp.bfloat16), 'head', scatter_dimensio...  43.9 us
    dot_general x1, matrix products, per_device(): jnp.dot(attended, out_weight, preferred_element_type=jnp.float32)  16.8 us
    all_gather x1, blocking collectives, per_device(): lax.all_gather(value_rows, 'seq', axis=0, tiled=True)  9.84 us
    all_gather x1, blocking collectives, per_device(): lax.all_gather(key_rows, 'seq', axis=0, tiled=True)  9.54 us
    psum x1, blocking collectives, per_device(): lax.psum(jnp.sum(widened * widened, axis=-1), 'head') / width_total  8.21 us
    unnamed x7, local copies, waits for them, and re-layouts  4.98 us
  transfers between devices with their start and end apart: 1, of which 1 were waited for; matrix products, arithmetic and copies ran while one was open for 0% of the time, Pallas kernels for 0%

profile of v2, /device:TPU:7, one launch (start us, length us, event | category | flops | bytes accessed | tf_op | source)
XLA Modules:
  0.0 218.1 jit_solution(14893291712828619165)
XLA Ops:
  7.2 0.0 reduce-scatter.2.cloned.1.call-start
  7.2 0.1 iota_compare_fusion
  7.3 1.0 copy.13
  8.3 9.5 %all_gather.6 = bf16[1024,256]{0,1:T(8,128)(2,1)S(1)} all-gather(bf16[128,256]{0,1:T(8,128)(2,1)S(1)} %copy.13), channel_id=1, replica_groups=mesh['seq'=8,'head'=4] {'seq'}, dimensions={0}, use_global_device_ids=true | all-gather | bytes 589824 | tf_op jit(solution)/shard_map/all_gather | solution.py:274
  17.8 1.1 copy.23
  19.0 9.8 %all_gather.7 = bf16[1024,256]{1,0:T(8,128)(2,1)S(1)} all-gather(bf16[128,256]{1,0:T(8,128)(2,1)} %param.10), channel_id=1, replica_groups=mesh['seq'=8,'head'=4] {'seq'}, dimensions={0}, use_global_device_ids=true | all-gather | bytes 589824 | tf_op jit(solution)/shard_map/all_gather | solution.py:275
  28.8 0.2 copy.16
  29.0 1.5 fusion.2
  30.5 1.7 fusion
  32.3 2.2 divide_convert_fusion
  34.4 0.0 copy-start.1
  34.5 16.8 %convolution_convert_fusion = bf16[128,8192]{1,0:T(8,128)(2,1)} fusion(bf16[128,2048]{0,1:T(8,128)(2,1)S(1)} %bitcast.38, bf16[2048,8192]{1,0:T(8,128)(2,1)} %param.11), kind=kOutput, calls=%fused_computation | convolution fusion | flops 4296015872 | bytes 36175872 | tf_op jit(solution)/shard_map/dot_general | solution.py:281
  51.3 0.0 reduce-scatter.2.cloned.1.call-update
  51.3 0.7 dynamic_slice.3
  52.0 43.9 %reduce-scatter.2.cloned.1.call-done = bf16[128,2048]{1,0:T(8,128)(2,1)} async-done(((bf16[128,8192]{1,0:T(8,128)(2,1)}), bf16[128,2048]{1,0:T(8,128)(2,1)}) %reduce-scatter.2.cloned.1.call-update) | async-done | bytes 524304 | tf_op jit(solution)/shard_map/reduce_scatter | solution.py:285
  95.9 0.0 copy-done.1
  95.9 1.3 fusion.9
  97.2 0.0 copy-start
  97.2 8.2 %psum.7 = f32[128]{0:T(128)S(1)} all-reduce(f32[128]{0:T(128)S(1)} %get-tuple-element.2), channel_id=1, replica_groups=mesh['seq'=8,'head'=4] {'head'}, use_global_device_ids=true, to_apply=%region_4.5 | all-reduce | flops 128 | bytes 1024 | tf_op jit(solution)/shard_map/psum | solution.py:290
  105.4 1.0 fusion.11.x_in
  106.4 102.0 %gather_and_project.1 = bf16[1024,896]{1,0:T(8,128)(2,1)} custom-call(bf16[128,2048]{1,0:T(8,128)(2,1)} %fusion.11.x_in, bf16[8192,896]{1,0:T(8,128)(2,1)} %gate_hbm.1, bf16[8192,896]{1,0:T(8,128)(2,1)} %up_hbm.1), custom_call_target="tpu_custom_call" | custom-call | flops 30064771072 | bytes 29360128 | tf_op jit(solution)/shard_map/gather_and_project/pallas_call | solution.py:213
  208.4 0.0 copy-done
  208.4 2.9 %copy.29 = bf16[1024,896]{1,0:T(8,128)(2,1)} copy(bf16[1024,896]{1,0:T(8,128)(2,1)} %gather_and_project.1) | data formatting | bytes 3670016
  (2 shorter events, 0.0 us)
Async XLA Ops:
  7.2 88.7 %reduce-scatter.2.cloned.1.call-start = ((), (), s32[]{:S(2)}) async-start(), calls=%async_computation.1 | async-start | bytes 2621440 | tf_op jit(solution)/shard_map/reduce_scatter | solution.py:285
  34.4 61.4 %copy-start.1 = (bf16[128,2048]{1,0:T(8,128)(2,1)S(1)}, bf16[128,2048]{1,0:T(8,128)(2,1)}, u32[]{:S(2)}) copy-start(bf16[128,2048]{1,0:T(8,128)(2,1)} %param.12) | copy-start | bytes 1572868
  97.2 111.2 %copy-start = (bf16[128,2048]{1,0:T(8,128)(2,1)}, bf16[128,2048]{1,0:T(8,128)(2,1)S(1)}, u32[]{:S(2)}) copy-start(bf16[128,2048]{1,0:T(8,128)(2,1)S(1)} %get-tuple-element.9) | copy-start | bytes 1572868
Sparse Core Ops, SparseCore 0:
  51.4 44.4 reduce-scatter.1
